TPU v7x, 32 devices: a whole 2x2x4 slice. The times are simulated.
32 devices in a mesh: req: 4 (over z), exp: 8 (over y, x, core).
Axes of the slice: x: 2, y: 2, z: 4, core: 2. Of those that a mesh axis runs over, the one named last changes fastest.
Arguments:
- hidden_in: bfloat16 [8, 512, 2048], P('exp'), may hold values from -6 to 6
- cache_keys: bfloat16 [8, 4096, 512], P('exp', None, 'req'), may hold values from -96 to 96
- cache_values: bfloat16 [8, 4096, 512], P('exp', None, 'req'), may hold values from -6 to 6
- cache_len: int32 [8], P('exp'), may hold values from 512 to 4096, as said below
- attn_gain: float32 [2048], replicated, may hold values from 0.25 to 1.75
- w_query: bfloat16 [2048, 4096], P('exp', 'req'), may hold values from -0.125 to 0.125
- w_key: bfloat16 [2048, 512], P('exp', 'req'), may hold values from -0.125 to 0.125
- w_value: bfloat16 [2048, 512], P('exp', 'req'), may hold values from -0.125 to 0.125
- q_gain: float32 [128], replicated, may hold values from 0.5 to 3
- k_gain: float32 [128], replicated, may hold values from 0.25 to 1.75
- w_out: bfloat16 [4096, 2048], P(('req', 'exp')), may hold values from -0.09375 to 0.09375
- moe_gain: float32 [2048], replicated, may hold values from 0.25 to 1.75
- expert_ids: int32 [8, 512, 8], P('exp', 'req'), may hold values from 0 to 31, all different within a row; in each aligned block of 128 rows (0 to 127, 128 to 255, ..., all dimensions but the last counted through in order) at most 48 rows name the same one
- expert_gates: float32 [8, 512, 8], P('exp', 'req'), may hold values from 0.05 to 0.5
- w_gate: bfloat16 [32, 2048, 768], P(('req', 'exp')), may hold values from -0.125 to 0.125
- w_up: bfloat16 [32, 2048, 768], P(('req', 'exp')), may hold values from -0.125 to 0.125
- w_down: bfloat16 [32, 768, 2048], P(('req', 'exp')), may hold values from -0.21875 to 0.21875
Outputs:
- hidden_out: bfloat16 [8, 512, 2048], P('exp', 'req')
- keys_out: bfloat16 [8, 4608, 512], P('exp', None, 'req')
- values_out: bfloat16 [8, 4608, 512], P('exp', None, 'req')
Inputs may be any that keep to these rules, and one draw needn't show every extreme that they name: `cache_len`: some request has exactly 4096 cached entries. `expert_ids`: each token names 8 different experts. In each aligned block of 128 tokens no expert is named more than 48 times, a bound that some block reaches.
All inputs are finite; a program needn't handle non-finite values.
Results may differ from a plain program's by a relative error of at most 0.014.
Values may be sent and summed in bfloat16 or wider, within the bound.
No kernel may reach another device: no remote copies, remote signals or barrier semaphores. Data moves between devices by JAX's collectives and lax.ppermute only.
A program may use at most 128 MiB of HBM per device.

v0:
```python
import jax
import jax.numpy as jnp
from jax import lax
from jax.sharding import PartitionSpec as P

EPS = 1e-06
THETA = 1000000.0


def rms_norm(values, gain_vec):
    values = values.astype(jnp.float32)
    factor = lax.rsqrt(jnp.mean(values * values, axis=-1, keepdims=True) + EPS)
    return values * factor * gain_vec


def rotate(values, positions):
    half_dim = values.shape[-1] // 2
    frequency = THETA ** (-jnp.arange(half_dim, dtype=jnp.float32) * 2.0 / values.shape[-1])
    angles = positions.astype(jnp.float32)[:, None] * frequency[None, :]
    cosine = jnp.cos(angles)[:, None, :]
    sine_part = jnp.sin(angles)[:, None, :]
    lower_half = values[..., :half_dim]
    upper_half = values[..., half_dim:]
    return jnp.concatenate(
        [
            lower_half * cosine - upper_half * sine_part,
            upper_half * cosine + lower_half * sine_part,
        ],
        axis=-1,
    )


def finish(query_proj, key_proj, value_proj, q_gain, k_gain, positions):
    stretch_len = query_proj.shape[0]
    head_dim = q_gain.shape[0]
    queries = rotate(
        rms_norm(query_proj.reshape(stretch_len, -1, head_dim), q_gain), positions
    ).astype(jnp.bfloat16)
    fresh_keys = rotate(
        rms_norm(key_proj.reshape(stretch_len, -1, head_dim), k_gain), positions
    ).astype(jnp.bfloat16)
    return (
        queries.transpose(1, 0, 2),
        fresh_keys.reshape(stretch_len, -1),
        value_proj.astype(jnp.bfloat16),
    )


def context(cache, fresh, head_dim):
    joined = jnp.concatenate([cache, fresh], axis=0)
    return joined.reshape(joined.shape[0], -1, head_dim).transpose(1, 0, 2)


def visible(length, context_len, stretch_len):
    key_pos = jnp.arange(context_len + stretch_len, dtype=jnp.int32)[None, :]
    query_pos = jnp.arange(stretch_len, dtype=jnp.int32)[:, None]
    return (key_pos < length) | (key_pos >= context_len) & (key_pos - context_len <= query_pos)


def attend(queries, keys, values, visible_mask):
    group_size = queries.shape[0] // keys.shape[0]
    score_scale = queries.shape[2] ** (-0.5)

    def one_head(operands):
        query_head, head_index = operands
        key_block = keys[head_index // group_size]
        value_block = values[head_index // group_size]
        scores = jnp.dot(query_head, key_block.T, preferred_element_type=jnp.float32) * score_scale
        scores = jnp.where(visible_mask, scores, -1e30)
        row_peak = jnp.max(scores, axis=1, keepdims=True)
        weights = jnp.where(visible_mask, jnp.exp(scores - row_peak), 0.0)
        running = jnp.sum(weights, axis=1, keepdims=True)
        mixed = jnp.dot(
            weights.astype(jnp.bfloat16), value_block, preferred_element_type=jnp.float32
        )
        return (mixed / running).astype(jnp.bfloat16)

    return lax.map(one_head, (queries, jnp.arange(queries.shape[0], dtype=jnp.int32)))


def append(cache, fresh, length):
    span = cache.shape[0] + fresh.shape[0]
    padded = jnp.concatenate([cache, jnp.zeros_like(fresh)], axis=0)
    kept_rows = jnp.where(
        (jnp.arange(span, dtype=jnp.int32) < length)[:, None], padded, jnp.zeros_like(padded)
    )
    return lax.dynamic_update_slice(kept_rows, fresh, (length, jnp.zeros((), jnp.int32)))


def body(
    hidden_in,
    cache_keys,
    cache_values,
    cache_len,
    attn_gain,
    w_query,
    w_key,
    w_value,
    q_gain,
    k_gain,
    w_out,
    moe_gain,
    expert_ids,
    expert_gates,
    w_gate,
    w_up,
    w_down,
):
    tokens = hidden_in[0]
    stretch_len = tokens.shape[0]
    model_width = tokens.shape[1]
    length = cache_len[0]
    head_dim = q_gain.shape[0]
    normed = rms_norm(tokens, attn_gain).astype(jnp.bfloat16)
    query_proj = jnp.dot(
        normed,
        lax.all_gather(w_query, "exp", axis=0, tiled=True),
        preferred_element_type=jnp.float32,
    )
    key_proj = jnp.dot(
        normed, lax.all_gather(w_key, "exp", axis=0, tiled=True), preferred_element_type=jnp.float32
    )
    value_proj = jnp.dot(
        normed,
        lax.all_gather(w_value, "exp", axis=0, tiled=True),
        preferred_element_type=jnp.float32,
    )
    positions = length + jnp.arange(stretch_len, dtype=jnp.int32)
    queries, fresh_keys, fresh_values = finish(
        query_proj, key_proj, value_proj, q_gain, k_gain, positions
    )
    context_len = cache_keys.shape[1]
    visible_mask = visible(length, context_len, stretch_len)
    attended = attend(
        queries,
        context(cache_keys[0], fresh_keys, head_dim),
        context(cache_values[0], fresh_values, head_dim),
        visible_mask,
    )
    attended = attended.transpose(1, 0, 2).reshape(stretch_len, -1)
    groups = lax.axis_size("req")
    row_count = stretch_len // groups
    offset = lax.axis_index("req") * row_count
    block_in = attended
    partial_out = jnp.dot(
        block_in,
        lax.all_gather(w_out, "exp", axis=0, tiled=True),
        preferred_element_type=jnp.float32,
    )
    mixed = lax.psum_scatter(
        partial_out.astype(jnp.bfloat16), "req", scatter_dimension=0, tiled=True
    ).astype(jnp.float32)
    resident = lax.dynamic_slice_in_dim(tokens, offset, row_count, 0)
    after_attn = (resident.astype(jnp.float32) + mixed).astype(jnp.bfloat16)
    moe_in = rms_norm(after_attn, moe_gain).astype(jnp.bfloat16)
    routes = expert_ids[0]
    top_k = routes.shape[1]
    experts = groups * lax.axis_size("exp")
    capacity = 3 * top_k * row_count // (2 * experts)
    flat_ids = routes.reshape(-1)
    onehot = (flat_ids[:, None] == jnp.arange(experts, dtype=jnp.int32)[None, :]).astype(jnp.int32)
    slots = jnp.sum((jnp.cumsum(onehot, axis=0) - 1) * onehot, axis=1)
    target = flat_ids * capacity + slots
    sources = jnp.arange(row_count * top_k, dtype=jnp.int32) // top_k
    outgoing = (
        jnp.zeros((experts * capacity, model_width), jnp.bfloat16).at[target].set(moe_in[sources])
    )
    outgoing = outgoing.reshape(experts, capacity, model_width)
    block_in = lax.all_to_all(outgoing, ("req", "exp"), split_axis=0, concat_axis=0, tiled=True)
    flat_rows = block_in.reshape(-1, model_width)
    gate_proj = jnp.dot(flat_rows, w_gate[0], preferred_element_type=jnp.float32)
    up_proj = jnp.dot(flat_rows, w_up[0], preferred_element_type=jnp.float32)
    activated = (jax.nn.silu(gate_proj) * up_proj).astype(jnp.bfloat16)
    produced = jnp.dot(activated, w_down[0], preferred_element_type=jnp.float32).astype(
        jnp.bfloat16
    )
    returned = lax.all_to_all(
        produced.reshape(block_in.shape), ("req", "exp"), split_axis=0, concat_axis=0, tiled=True
    )
    picked = returned.reshape(experts * capacity, model_width)[target].reshape(
        row_count, top_k, model_width
    )
    combined = jnp.sum(picked.astype(jnp.float32) * expert_gates[0][:, :, None], axis=1)
    result_rows = (after_attn.astype(jnp.float32) + combined).astype(jnp.bfloat16)
    keys_out = append(cache_keys[0], fresh_keys, length)
    values_out = append(cache_values[0], fresh_values, length)
    return (result_rows[None], keys_out[None], values_out[None])


def solution(mesh):
    placed = (
        P("exp", None, None),
        P("exp", None, "req"),
        P("exp", None, "req"),
        P("exp"),
        P(),
        P("exp", "req"),
        P("exp", "req"),
        P("exp", "req"),
        P(),
        P(),
        P(("req", "exp"), None),
        P(),
        P("exp", "req", None),
        P("exp", "req", None),
        P(("req", "exp"), None, None),
        P(("req", "exp"), None, None),
        P(("req", "exp"), None, None),
    )
    return jax.shard_map(
        body,
        mesh=mesh,
        in_specs=placed,
        out_specs=(P("exp", "req", None), P("exp", None, "req"), P("exp", None, "req")),
        check_vma=False,
    )
```

profile of v0, /device:TPU:0, one launch (start us, length us, event | category | flops | bytes accessed | tf_op | source)
XLA Modules:
  0.0 584.7 jit_solution(6654928557229151965)
XLA Ops:
  11.6 11.6 %all_gather.13 = bf16[2048,128]{1,0:T(8,128)(2,1)S(1)} all-gather(bf16[256,128]{1,0:T(8,128)(2,1)} %param.25), channel_id=1, replica_groups=mesh['req'=4,'exp'=8] {'exp'}, dimensions={0}, use_global_device_ids=true | all-gather | bytes 589824 | tf_op jit(solution)/shard_map/all_gather | solution.py:121
  28.4 11.4 %all_gather.14 = bf16[2048,128]{1,0:T(8,128)(2,1)S(1)} all-gather(bf16[256,128]{1,0:T(8,128)(2,1)S(1)} %copy-done.13), channel_id=1, replica_groups=mesh['req'=4,'exp'=8] {'exp'}, dimensions={0}, use_global_device_ids=true | all-gather | bytes 589824 | tf_op jit(solution)/shard_map/all_gather | solution.py:125
  42.2 7.9 %select_bitcast_fusion = (bf16[1,4608,128]{2,1,0:T(8,128)(2,1)}, bf16[1,4608,128]{2,1,0:T(8,128)(2,1)}, bf16[1,4608,128]{2,1,0:T(8,128)(2,1)}, bf16[1,4608,128]{2,1,0:T(8,128)(2,1)}) fusion(bf16[4096,128]{1,0:T(8,128)(2,1)} %bitcast.136, pred[4608]{0:T(1024)(128)(4,1)S(1)} %get-tuple-element.187, bf16[512,128]{1,0:T(8,128)(2,1)S(1)} %convolution_convert_fusion.2, ...), kind=kLoop, calls=%fused_computation.58 | loop fusion | flops 5898240 | bytes 7082496 | tf_op jit(solution)/shard_map/broadcast_in_dim | solution.py:187
  50.1 6.5 %copy.25 = bf16[1024,2048]{1,0:T(8,128)(2,1)} copy(bf16[1024,2048]{0,1:T(8,128)(2,1)} %bitcast.134) | data formatting | bytes 8388608 | tf_op jit(solution)/shard_map/dot_general | solution.py:115
  56.6 5.5 multiply_reduce_fusion
  64.5 111.1 %while.12 = (s32[]{:T(128)}, bf16[8,512,128]{1,2,0:T(8,128)(2,1)}, bf16[8,512,128]{1,2,0:T(8,128)(2,1)}, bf16[1,4608,128]{2,1,0:T(8,128)(2,1)}, bf16[1,4608,128]...) while((s32[]{:T(128)}, bf16[8,512,128]{1,2,0:T(8,128)(2,1)}, ...), condition=%wide.region_6.7_spmd.clone, body=%wide.region_3.6_spmd.clone.sunk | while | flops 1259994112 | bytes 36270200 | solution.py:78
  69.2 4.9 fusion.90
  83.1 4.9 fusion.90
  96.9 4.9 fusion.90
  110.8 4.9 fusion.90
  124.7 4.9 fusion.90
  138.5 4.9 fusion.90
  152.4 4.9 fusion.90
  175.6 6.2 %convolution_convert_fusion.1 = bf16[512,2048]{1,0:T(8,128)(2,1)} fusion(bf16[512,1024]{0,1:T(8,128)(2,1)} %bitcast.150, bf16[1024,2048]{1,0:T(8,128)(2,1)} %all-gather.5.cloned.1.call-done), kind=kOutput, calls=%fused_computation.46 | convolution fusion | flops 2148532224 | bytes 7340032 | tf_op jit(solution)/shard_map/dot_general | solution.py:145
  182.2 9.4 %reduce-window.6 = s32[32,8,128]{2,1,0:T(8,128)S(1)} reduce-window(s32[32,8,128]{2,1,0:T(8,128)S(1)} %fusion.72, s32[]{:T(128)} %constant.96.clone.1), window={size=1x1x128 pad=0_0x0_0x127_0}, to_apply=%region_8.9 | reduce-window | flops 4161536 | bytes 262148 | tf_op jit(solution)/shard_map/reduce-window
  192.4 33.7 %reduce-scatter.2.cloned.1.call-done = bf16[128,2048]{1,0:T(8,128)(2,1)} async-done(((bf16[512,2048]{1,0:T(8,128)(2,1)}), bf16[128,2048]{1,0:T(8,128)(2,1)}) %reduce-scatter.2.cloned.1.call-update) | async-done | bytes 524304 | tf_op jit(solution)/shard_map/reduce_scatter | solution.py:150
  229.3 24.2 %scatter_custom_fusion = bf16[1536,2048]{1,0:T(8,128)(2,1)} fusion(s32[1024]{0:T(1024)S(1)} %bitcast.146, bf16[128,2048]{1,0:T(8,128)(2,1)} %fusion.55, s32[1024]{0:T(1024)S(1)} %broadcast_clamp_fusion.1, bf16[]{:T(256)} %constant.100.clone.1), kind=kCustom, calls=%fused_computation.39 | custom fusion | bytes 6291968 | tf_op jit(solution)/shard_map/scatter | solution.py:166
  253.5 142.5 %all_to_all.10 = bf16[32,48,2048]{2,1,0:T(8,128)(2,1)S(1)} all-to-all(bf16[32,48,2048]{2,1,0:T(8,128)(2,1)} %bitcast.130), channel_id=1, replica_groups=mesh['req'=4,'exp'=8] {'req','exp'}, dimensions={0} | all-to-all | bytes 12582912 | tf_op jit(solution)/shard_map/all_to_all | solution.py:169
  396.1 5.2 fusion.45
  401.3 5.6 multiply_convert_fusion
  406.9 7.1 %convolution_convert_fusion = bf16[1536,2048]{1,0:T(8,128)(2,1)} fusion(bf16[1536,768]{1,0:T(8,128)(2,1)S(1)} %multiply_convert_fusion, bf16[1,768,2048]{2,1,0:T(8,128)(2,1)S(1)} %copy-done), kind=kOutput, calls=%fused_computation.28 | convolution fusion | flops 4834983936 | bytes 11796480 | tf_op jit(solution)/shard_map/dot_general | solution.py:174
  422.3 135.7 %all-to-all-done.1 = bf16[32,48,2048]{2,1,0:T(8,128)(2,1)} async-done(((bf16[32,48,2048]{2,1,0:T(8,128)(2,1)}), bf16[32,48,2048]{2,1,0:T(8,128)(2,1)}, u32[]{:S(2)}, u32[]{:S(2)}) %all-to-all-start.1) | async-done | bytes 6291488 | tf_op jit(solution)/shard_map/all_to_all | solution.py:177
  558.1 12.4 %gather_fusion = bf16[1024,2048]{1,0:T(8,128)(2,1)} fusion(bf16[1536,2048]{1,0:T(8,128)(2,1)} %bitcast.28, s32[1024]{0:T(1024)S(1)} %broadcast_clamp_fusion), kind=kCustom, calls=%fused_computation.1 | custom fusion | bytes 8392704 | tf_op jit(solution)/shard_map/gather | solution.py:180
  570.5 6.6 %fusion.33 = f32[128,2048]{1,0:T(8,128)S(1)} fusion(bf16[1024,2048]{1,0:T(8,128)(2,1)} %gather_fusion, f32[128,8]{1,0:T(8,128)S(1)} %copy-done.12), kind=kLoop, calls=%fused_computation.27 | loop fusion | flops 6029312 | bytes 5246976 | tf_op jit(solution)/shard_map/reduce_sum | solution.py:183
  (146 shorter events, 103.4 us)
Async XLA Ops:
  7.2 399.7 %copy-start = (bf16[1,768,2048]{2,1,0:T(8,128)(2,1)S(1)}, bf16[1,768,2048]{2,1,0:T(8,128)(2,1)}, u32[]{:S(2)}) copy-start(bf16[1,768,2048]{2,1,0:T(8,128)(2,1)} %param.35) | copy-start | bytes 9437188
  7.2 19.7 %copy-start.17 = (f32[128]{0:T(128)S(1)}, f32[128]{0:T(128)}, u32[]{:S(2)}) copy-start(f32[128]{0:T(128)} %param.28) | copy-start | bytes 1540
  7.2 42.9 %all-gather.3.cloned.1.call-start = ((), (), s32[]{:S(2)}) async-start(), calls=%async_computation.3 | async-start | bytes 4718592 | tf_op jit(solution)/shard_map/all_gather | solution.py:117
  7.9 167.7 %all-gather.5.cloned.1.call-start = ((), (), s32[]{:S(2)}) async-start(), calls=%async_computation.4 | async-start | bytes 4718592 | tf_op jit(solution)/shard_map/all_gather | solution.py:147
  8.7 217.4 %reduce-scatter.2.cloned.1.call-start = ((), (), s32[]{:S(2)}) async-start(), calls=%async_computation.5 | async-start | bytes 2621440 | tf_op jit(solution)/shard_map/reduce_scatter | solution.py:150
  9.4 19.0 %copy-start.13 = (bf16[256,128]{1,0:T(8,128)(2,1)S(1)}, bf16[256,128]{1,0:T(8,128)(2,1)}, u32[]{:S(2)}) copy-start(bf16[256,128]{1,0:T(8,128)(2,1)} %param.26) | copy-start | bytes 196612
  9.4 30.4 %copy-start.21 = (f32[2048]{0:T(1024)S(1)}, f32[2048]{0:T(1024)}, u32[]{:S(2)}) copy-start(f32[2048]{0:T(1024)} %param.23) | copy-start | bytes 24580
  42.2 14.4 %copy-start.8 = (bf16[512,128]{1,0:T(8,128)(2,1)}, bf16[512,128]{1,0:T(8,128)(2,1)S(1)}, u32[]{:S(2)}) copy-start(bf16[512,128]{1,0:T(8,128)(2,1)S(1)} %convolution_convert_fusion.2) | copy-start | bytes 393220
  56.6 5.5 copy-start.18
  69.2 4.9 copy-start.3
  83.1 4.9 copy-start.3
  96.9 4.9 copy-start.3
  110.8 4.9 copy-start.3
  124.7 4.9 copy-start.3
  138.5 4.9 copy-start.3
  152.4 4.9 copy-start.3
  175.6 6.3 %copy-start.14 = (s32[1,128,8]{1,2,0:T(8,128)S(1)}, s32[1,128,8]{1,2,0:T(8,128)}, u32[]{:S(2)}) copy-start(s32[1,128,8]{1,2,0:T(8,128)} %param.31) | copy-start | bytes 12292
  181.8 46.5 %copy-start.15 = (f32[2048]{0:T(1024)S(1)}, f32[2048]{0:T(1024)}, u32[]{:S(2)}) copy-start(f32[2048]{0:T(1024)} %param.30) | copy-start | bytes 24580
  253.5 142.5 %copy-start.19 = (bf16[1,2048,768]{2,1,0:T(8,128)(2,1)S(1)}, bf16[1,2048,768]{2,1,0:T(8,128)(2,1)}, u32[]{:S(2)}) copy-start(bf16[1,2048,768]{2,1,0:T(8,128)(2,1)} %param.33) | copy-start | bytes 9437188
  396.1 5.2 copy-start.20
  414.0 6.7 %copy-start.9 = (bf16[512,128]{1,0:T(8,128)(2,1)S(1)}, bf16[512,128]{1,0:T(8,128)(2,1)}, u32[]{:S(2)}) copy-start(bf16[512,128]{1,0:T(8,128)(2,1)} %copy-done.8) | copy-start | bytes 393220
  414.0 144.1 %all-to-all-start.1 = ((bf16[32,48,2048]{2,1,0:T(8,128)(2,1)}), bf16[32,48,2048]{2,1,0:T(8,128)(2,1)}, u32[]{:S(2)}, u32[]{:S(2)}) async-start(bf16[32,48,2048]{2,1,0:T(8,128)(2,1)} %bitcast.131), calls=%async_computation.2 | async-start | bytes 12582912 | tf_op jit(solution)/shard_map/all_to_all | solution.py:177
  558.1 12.4 %copy-start.12 = (f32[128,8]{1,0:T(8,128)S(1)}, f32[128,8]{1,0:T(8,128)}, u32[]{:S(2)}) copy-start(f32[128,8]{1,0:T(8,128)} %copy.34) | copy-start | bytes 12292
  570.5 6.6 %copy-start.2 = (bf16[128,2048]{1,0:T(8,128)(2,1)S(1)}, bf16[128,2048]{1,0:T(8,128)(2,1)}, u32[]{:S(2)}) copy-start(bf16[128,2048]{1,0:T(8,128)(2,1)} %copy-done.1) | copy-start | bytes 1572868
  (9 other events, 22.7 us)
Sparse Core Ops, SparseCore 0:
  9.9 40.1 all-gather.2
  52.0 36.8 all-gather.4
  182.0 44.0 reduce-scatter.1
where the time goes:
time: 593 us; the launch traced here: 585 us
  waiting for transfers between devices  171 us (29%)
  blocking collectives  166 us (28%)
  matrix products  99.6 us (17%)
  other arithmetic  72.5 us (12%)
  local copies, waits for them, and re-layouts  56.5 us (10%)
  between operations  15 us (3%)
    all_to_all x1, blocking collectives, body(): lax.all_to_all(outgoing, ('req', 'exp'), split_axis=0, concat_axis=0, til...  143 us
    all_to_all x1, waiting for transfers between devices, body(): lax.all_to_all(produced.reshape(block_in.shape), ('req', 'exp'), split_ax...  136 us
    reduce_sum x8, other arithmetic, one_head(): running = jnp.sum(weights, axis=1, keepdims=True)  39.1 us
    dot_general x8, matrix products, one_head(): jnp.dot(query_head, key_block.T, preferred_element_type=jnp.float32)  35.7 us
    reduce_scatter x1, waiting for transfers between devices, body(): lax.psum_scatter(partial_out.astype(jnp.bfloat16), 'req', scatter_dimensi...  33.7 us
    dot_general x8, matrix products, one_head(): jnp.dot(weights.astype(jnp.bfloat16), value_block, preferred_element_type...  29.4 us
    scatter x1, local copies, waits for them, and re-layouts, body(): jnp.zeros((experts * capacity, model_width), jnp.bfloat16).at[target]  24.2 us
    gather x1, local copies, waits for them, and re-layouts, body(): returned.reshape(experts * capacity, model_width)[target]  12.4 us
  transfers between devices with their start and end apart: 4, of which 2 were waited for; matrix products, arithmetic and copies ran while one was open for 27% of the time, Pallas kernels for 0%

commit v1 on v0

v1 whole, which is shorter than its diff:
```python
import functools
import math

import jax
import jax.numpy as jnp
from jax import lax
from jax.experimental import pallas as pl
from jax.experimental.pallas import tpu as pltpu
from jax.sharding import PartitionSpec as P

EPS = 1e-06
THETA = 1000000.0
ROWS = 128
ORDER = (0, 2, 1, 3)
HIDE = -1e30
KEYS = 512
TILE = 256
PICK = 384
CHUNKS = (64, 64)
WIDE = 1024
MB = 1024 * 1024
F32 = jnp.float32
BF16 = jnp.bfloat16

VMEM = pltpu.VMEM
SMEM = pltpu.SMEM
HBM = pltpu.HBM


def spec(space):
    return pl.BlockSpec(memory_space=space)


def params(limit_mb):
    return pltpu.CompilerParams(vmem_limit_bytes=limit_mb * MB)


def swap(value, bit, size):
    return lax.ppermute(value, "exp", [(i, i ^ bit) for i in range(size)])


def shift(value, step, size):
    return lax.ppermute(value, "req", [(i, (i + step) % size) for i in range(size)])


def chip_bits(size):
    bits, bit = [], 2
    while bit < size:
        bits.append(bit)
        bit *= 2
    return bits


def spread(value, size):
    half = value.shape[0] // 2
    if size == 8:
        x, y = swap(value, 2, size), swap(value, 4, size)
        first, second = swap(x[:half], 4, size), swap(y[half:], 2, size)
        out = [(0, 0, value), (2, 0, x), (4, 0, y), (6, 0, first), (6, half, second)]
    else:
        out = []
        for start in (0, half):
            held = {0: value[start : start + half]}
            for bit in chip_bits(size) if start == 0 else chip_bits(size)[::-1]:
                held.update({b ^ bit: swap(v, bit, size) for b, v in list(held.items())})
            out += [(b, start, v) for b, v in held.items()]
    return out + [(b ^ 1, start, swap(v, 1, size)) for b, start, v in out]


def add(*terms):
    total = terms[0].astype(F32)
    for term in terms[1:]:
        total = total + term.astype(F32)
    return total.astype(BF16)


def gather_sums(parts, size):
    half = parts[0].shape[0] // 2
    both = {b: (parts[b], swap(parts[b ^ 1], 1, size)) for b in (6, 4, 2, 0)}
    first = add(*(v[:half] for v in both[6]))
    second = add(*(v[half:] for v in both[6]))
    first, second = swap(first, 2, size), swap(second, 4, size)
    y = jnp.concatenate([add(*(v[:half] for v in both[4]), first), add(*(v[half:] for v in both[4]))])
    x = jnp.concatenate([add(*(v[:half] for v in both[2])), add(*(v[half:] for v in both[2]), second)])
    return both[0] + (swap(x, 2, size), swap(y, 4, size)), [v[1] for v in both.values()]


def along(value, pairs):
    return lax.ppermute(value, "req", pairs)


def along_sum(parts, z, groups):
    if groups != 4:
        return [parts[0]] + [shift(parts[k], k, groups) for k in range(1, groups)]
    up = along(parts[1], [(0, 1), (1, 2), (2, 3)])
    down = along(parts[3], [(1, 0), (2, 1), (3, 2)])
    relayed = along(parts[4], [(0, 1), (3, 2)])
    over = along(add(parts[2], relayed), [(0, 2), (1, 3), (2, 0), (3, 1)])
    return [parts[0], up, down, over]


def along_gather(value, z, groups):
    over = along(value, [(0, 2), (1, 3), (2, 0), (3, 1)])
    up = along(value, [(0, 1), (1, 2), (2, 3)])
    down = along(value, [(1, 0), (2, 1), (3, 2)])
    relayed = along(over, [(1, 0), (2, 3)])
    got = [value, jnp.where(z == 0, relayed, up), over, jnp.where(z == 3, relayed, down)]
    return jnp.concatenate([got[k] for k in ORDER])


def stage_kernel(w_ref, *rest):
    rest[-1][...] = w_ref[...]


def stage(w, extra):
    return pl.pallas_call(
        stage_kernel,
        out_shape=jax.ShapeDtypeStruct(w.shape, w.dtype),
        in_specs=[spec(VMEM)] + [spec(HBM)] * len(extra),
        out_specs=spec(VMEM),
        name="stage",
    )(w, *extra)


def start_loads(e, pieces, at, shard, w_ref, sem):
    copies = []
    for i, (piece, (b, start)) in enumerate(zip(pieces, at)):
        row = pl.multiple_of((e ^ b) * shard + start, 16)
        copy = pltpu.make_async_copy(piece, w_ref.at[pl.ds(row, piece.shape[0])], sem.at[i])
        copy.start()
        copies.append(copy)
    return copies


def project_kernel(marks, x_ref, gain_ref, cos_ref, sin_ref, qg_ref, kg_ref, *rest, at, shard, heads, chunks, groups):
    pieces, rest = rest[: len(at)], rest[len(at) :]
    q_refs, rest = rest[: len(chunks)], rest[len(chunks) :]
    k_ref, v_ref, w_ref, n_ref, sem = rest
    copies = start_loads(marks[1], pieces, at, shard, w_ref, sem)
    x = x_ref[...].astype(F32)
    factor = lax.rsqrt(jnp.mean(x * x, axis=-1, keepdims=True) + EPS)
    n_ref[...] = (x * factor * gain_ref[...]).astype(BF16)
    for copy in copies:
        copy.wait()
    hd = qg_ref.shape[1]
    starts = [sum(chunks[:c]) for c in range(len(chunks))]

    def turned(value, gain):
        factor = lax.rsqrt(jnp.mean(value * value, axis=-1, keepdims=True) + EPS)
        value = value * factor * gain
        return value * cos_ref[...] + pltpu.roll(value, hd // 2, 1) * sin_ref[...]

    scale = hd ** (-0.5) * math.log2(math.e)

    for first in range(0, heads, 4):
        four = jnp.dot(n_ref[...], w_ref[:, first * hd : (first + 4) * hd], preferred_element_type=F32)
        for s in range(4):
            q = (turned(four[:, s * hd : (s + 1) * hd], qg_ref[...]) * scale).astype(BF16)
            for c, rows in enumerate(chunks):
                span = groups * rows
                q_refs[c][(first + s) * span : (first + s + 1) * span] = q[starts[c] * groups :][:span]
    both = jnp.dot(n_ref[...], w_ref[:, heads * hd : (heads + 2) * hd], preferred_element_type=F32)
    k = turned(both[:, :hd], kg_ref[...]).astype(BF16)
    v = both[:, hd:].astype(BF16)
    for c, rows in enumerate(chunks):
        for r in range(groups):
            src = slice(starts[c] * groups + r * rows, starts[c] * groups + (r + 1) * rows)
            dst = slice(r * ROWS + starts[c], r * ROWS + starts[c] + rows)
            k_ref[dst] = k[src]
            v_ref[dst] = v[src]


def project(marks, x, gain, cos, sin, q_gain, k_gain, pieces, size, heads, chunks, groups):
    tokens, width = x.shape
    hd = q_gain.shape[1]
    at = [piece[:2] for piece in pieces]
    pieces = [piece[2] for piece in pieces]
    cols = pieces[0].shape[1]
    return pl.pallas_call(
        functools.partial(project_kernel, at=at, shard=width // size, heads=heads, chunks=chunks, groups=groups),
        out_shape=(
            *(jax.ShapeDtypeStruct((heads * groups * rows, hd), BF16) for rows in chunks),
            jax.ShapeDtypeStruct((tokens, hd), BF16),
            jax.ShapeDtypeStruct((tokens, hd), BF16),
        ),
        in_specs=[spec(SMEM)] + [spec(VMEM)] * 6 + [spec(HBM)] * len(pieces),
        out_specs=(spec(VMEM),) * (2 + len(chunks)),
        scratch_shapes=[
            VMEM((width, cols), BF16),
            VMEM((tokens, width), BF16),
            pltpu.SemaphoreType.DMA((len(pieces),)),
        ],
        compiler_params=params(40),
        cost_estimate=pl.CostEstimate(flops=2 * tokens * width * cols, bytes_accessed=10 * MB, transcendentals=0),
        name="project",
    )(marks, x, gain, cos, sin, q_gain, k_gain, *pieces)


def attend_kernel(marks, q_hbm, kc_hbm, vc_hbm, kn_hbm, vn_hbm, *rest, start, rows, heads):
    o_ref, marks_out, qa, ka, va, s0, s1, m0, m1, bias, sem = rest[-11:]
    ctx, hd = kc_hbm.shape
    keys = ctx + kn_hbm.shape[0]
    tokens = qa.shape[0] // heads
    loads = [
        pltpu.make_async_copy(src, dst, sem.at[i])
        for i, (src, dst) in enumerate(
            (
                (q_hbm, qa.at[:, :hd]),
                (kc_hbm, ka.at[:ctx, :hd]),
                (kn_hbm, ka.at[ctx:, :hd]),
                (vc_hbm, va.at[:ctx, :hd]),
                (vn_hbm, va.at[ctx:, :hd]),
            )
        )
    ]
    for load in loads:
        load.start()
    for i in range(3):
        marks_out[i] = marks[i]
    length = marks[0]
    lane = lax.broadcasted_iota(jnp.int32, (1, hd), 1)
    qa[:, hd:] = jnp.broadcast_to(jnp.where(lane == 0, 1.0, 0.0), (heads * tokens, hd)).astype(BF16)
    where = lax.broadcasted_iota(jnp.int32, (keys, hd), 0)
    first = lax.broadcasted_iota(jnp.int32, (keys, hd), 1) == 0
    ka[:, hd:] = jnp.where(first & (where >= length) & (where < ctx), HIDE, 0.0).astype(BF16)
    va[:, hd:] = jnp.ones((keys, hd), BF16)
    tile = bias.shape[0]
    at = lax.broadcasted_iota(jnp.int32, (tile, KEYS), 0) % tokens
    token = (at // rows) * ROWS + start + at % rows
    bias[...] = jnp.where(lax.broadcasted_iota(jnp.int32, (tile, KEYS), 1) <= token, 0.0, HIDE)
    blocks = keys // KEYS
    tiles = heads * tokens // tile
    per = tile // tokens

    for load in loads:
        load.wait()

    def scores(i, buf, j, peak):
        q = qa[pl.ds(pl.multiple_of(i * tile, tile), tile)]
        s = lax.dot_general(q, ka[j * KEYS : (j + 1) * KEYS], (((1,), (1,)), ((), ())), preferred_element_type=F32)
        if j == blocks - 1:
            s = s + bias[...]
        buf[:, j * KEYS : (j + 1) * KEYS] = s
        for c in range(KEYS // hd):
            part = s[:, c * hd : (c + 1) * hd]
            peak = part if peak is None else jnp.maximum(peak, part)
        return peak

    def top(peak):
        return jnp.broadcast_to(jnp.max(peak, axis=1, keepdims=True), (tile, hd))

    def mix(buf, m_ref, j, total):
        m = m_ref[...]
        s = buf[:, j * KEYS : (j + 1) * KEYS]
        p = jnp.concatenate(
            [jnp.exp2(s[:, c * hd : (c + 1) * hd] - m).astype(BF16) for c in range(KEYS // hd)], axis=1
        )
        part = jnp.dot(p, va[j * KEYS : (j + 1) * KEYS], preferred_element_type=F32)
        return part if total is None else total + part

    def finish(i, total):
        out = (total[:, :hd] / total[:, hd:]).astype(BF16)
        for h in range(per):
            o_ref[i * per + h] = out[h * tokens : (h + 1) * tokens]

    bufs, peaks = (s0, s1), (m0, m1)

    def step(i, parity, score, mixing):
        peak = total = None
        for j in range(blocks):
            if score:
                peak = scores(i, bufs[parity], j, peak)
            if mixing:
                total = mix(bufs[1 - parity], peaks[1 - parity], j, total)
        if score:
            peaks[parity][...] = top(peak)
        if mixing:
            finish(i - 1, total)

    step(0, 0, True, False)
    step(1, 1, True, True)

    def two(n, carry):
        step(2 * n, 0, True, True)
        step(2 * n + 1, 1, True, True)
        return carry

    lax.fori_loop(1, tiles // 2, two, 0)
    step(tiles, 0, False, True)


def attend(marks, q, kc, vc, kn, vn, start, rows, heads, extra=()):
    hd = q.shape[1]
    tokens = q.shape[0] // heads
    keys = kc.shape[0] + kn.shape[0]
    tile = tokens * max(1, TILE // tokens)
    return pl.pallas_call(
        functools.partial(attend_kernel, start=start, rows=rows, heads=heads),
        out_shape=(jax.ShapeDtypeStruct((heads, tokens, hd), BF16), jax.ShapeDtypeStruct((3,), jnp.int32)),
        in_specs=[spec(SMEM)] + [spec(HBM)] * (5 + len(extra)),
        out_specs=(spec(VMEM), spec(SMEM)),
        scratch_shapes=[
            VMEM((heads * tokens, 2 * hd), BF16),
            VMEM((keys, 2 * hd), BF16),
            VMEM((keys, 2 * hd), BF16),
            VMEM((tile, keys), F32),
            VMEM((tile, keys), F32),
            VMEM((tile, hd), F32),
            VMEM((tile, hd), F32),
            VMEM((tile, KEYS), F32),
            pltpu.SemaphoreType.DMA((5,)),
        ],
        compiler_params=params(40),
        cost_estimate=pl.CostEstimate(
            flops=8 * heads * tokens * keys * hd, bytes_accessed=4 * MB, transcendentals=heads * tokens * keys
        ),
        name="attend",
    )(marks, q, kc, vc, kn, vn, *extra)


def out_kernel(marks, att_ref, *rest, at, shard, groups):
    pieces, rest = rest[: len(at)], rest[len(at) :]
    outs, (w_ref, o_ref, sem) = rest[:-3], rest[-3:]
    copies = start_loads(marks[1], pieces, at, shard, w_ref, sem)
    heads, tokens, hd = att_ref.shape
    att = jnp.concatenate([att_ref[h] for h in range(heads)], axis=1)
    for copy in copies:
        copy.wait()
    rows = tokens // groups

    for n in range(0, w_ref.shape[1], WIDE):
        cols = slice(n, n + WIDE)
        part = jnp.dot(att, w_ref[:, cols], preferred_element_type=F32).astype(BF16)
        for r in range(groups):
            o_ref[r, :, cols] = part[r * rows : (r + 1) * rows]
    for k in range(groups):
        outs[k][...] = o_ref[lax.rem(marks[2] + k, groups)]
    outs[groups][...] = o_ref[jnp.where(marks[2] == 0, groups - 1, 0)]


def out_project(marks, att, pieces, size, groups):
    heads, tokens, hd = att.shape
    at = [piece[:2] for piece in pieces]
    pieces = [piece[2] for piece in pieces]
    width = pieces[0].shape[1]
    rows = tokens // groups
    return pl.pallas_call(
        functools.partial(out_kernel, at=at, shard=heads * hd // size, groups=groups),
        out_shape=(jax.ShapeDtypeStruct((rows, width), BF16),) * (groups + 1),
        in_specs=[spec(SMEM), spec(VMEM)] + [spec(HBM)] * len(pieces),
        out_specs=(spec(VMEM),) * (groups + 1),
        scratch_shapes=[
            VMEM((heads * hd, width), BF16),
            VMEM((groups, rows, width), BF16),
            pltpu.SemaphoreType.DMA((len(pieces),)),
        ],
        compiler_params=params(24),
        cost_estimate=pl.CostEstimate(flops=2 * tokens * heads * hd * width, bytes_accessed=5 * MB, transcendentals=0),
        name="out_project",
    )(marks, att, *pieces)


def norm_kernel(x_ref, gain_ref, *rest):
    parts, (after_ref, moe_ref) = rest[:-2], rest[-2:]
    total = parts[0][...].astype(F32)
    for part in parts[1:]:
        total = total + part[...].astype(F32)
    after = (x_ref[...].astype(F32) + total).astype(BF16)
    after_ref[...] = after
    x = after.astype(F32)
    factor = lax.rsqrt(jnp.mean(x * x, axis=-1, keepdims=True) + EPS)
    moe_ref[...] = (x * factor * gain_ref[...]).astype(BF16)


def add_norm(x, gain, parts):
    shape = jax.ShapeDtypeStruct(x.shape, BF16)
    return pl.pallas_call(
        norm_kernel,
        out_shape=(shape, shape),
        in_specs=[spec(VMEM)] * (2 + len(parts)),
        out_specs=(spec(VMEM),) * 2,
        name="add_norm",
    )(x, gain, *parts)


def expert_kernel(count_ref, slot_ref, gate_ref, *rest, at, span, extras):
    pieces, rest = rest[: len(at)], rest[len(at) :]
    wg_hbm, wu_hbm, wd_hbm = rest[:3]
    outs = rest[3 + extras : -8]
    x_ref, wg, wu, wd, xg, hid, sem, wsem = rest[-8:]
    copies = []
    for i, (piece, (b, start)) in enumerate(zip(pieces, at)):
        row = b * span + start
        copy = pltpu.make_async_copy(piece, x_ref.at[row : row + piece.shape[0]], sem.at[i])
        copy.start()
        copies.append(copy)
    loads = []
    for i, (src, dst) in enumerate(((wg_hbm, wg), (wu_hbm, wu), (wd_hbm, wd))):
        copy = pltpu.make_async_copy(src, dst, wsem.at[i])
        copy.start()
        loads.append(copy)
    tokens, width = x_ref.shape
    slots = slot_ref[...]
    slots_t = jnp.transpose(jnp.broadcast_to(slots, (128, tokens)))

    def tile(base, first):
        slot = lax.broadcasted_iota(jnp.int32, (PICK, tokens), 0).astype(F32) + base
        hit = slot == slots
        pick = jnp.where(hit, 1.0, 0.0).astype(BF16)
        gate = jnp.sum(jnp.where(hit, gate_ref[...], 0.0), axis=1, keepdims=True)
        lane = lax.broadcasted_iota(jnp.int32, (tokens, 128), 1).astype(F32) + base
        put = jnp.concatenate(
            [jnp.where(lane + n == slots_t, 1.0, 0.0).astype(BF16) for n in range(0, PICK, 128)], axis=1
        )
        if first:
            for copy in copies:
                copy.wait()
        for n in range(0, width, WIDE):
            cols = slice(n, n + WIDE)
            xg[:, cols] = jnp.dot(pick, x_ref[:, cols], preferred_element_type=F32).astype(BF16)
        if first:
            loads[0].wait()
            loads[1].wait()
        g = jnp.dot(xg[...], wg[...], preferred_element_type=F32)
        u = jnp.dot(xg[...], wu[...], preferred_element_type=F32)
        hid[...] = (g / (1.0 + jnp.exp(-g)) * u).astype(BF16)
        if first:
            loads[2].wait()
        for n in range(0, width, WIDE):
            cols = slice(n, n + WIDE)
            o = jnp.dot(hid[...], wd[:, cols], preferred_element_type=F32).astype(BF16)
            o = (o.astype(F32) * gate).astype(BF16)
            back = jnp.dot(put, o, preferred_element_type=F32).astype(BF16)
            for i, out in enumerate(outs):
                part = back[i * span : (i + 1) * span]
                out[:, cols] = part if first else out[:, cols] + part

    tile(0.0, True)

    def more(i, carry):
        tile((i * PICK).astype(F32), False)
        return carry

    lax.fori_loop(1, lax.div(count_ref[0] + (PICK - 1), PICK), more, 0)


def experts(count, slots, gate, pieces, wg, wu, wd, extra, size):
    at = [piece[:2] for piece in pieces]
    pieces = [piece[2] for piece in pieces]
    span, width = pieces[0].shape
    tokens = size * span
    n = len(pieces)
    ff = wg.shape[1]
    return pl.pallas_call(
        functools.partial(expert_kernel, at=at, span=span, extras=len(extra)),
        out_shape=(jax.ShapeDtypeStruct((span, width), BF16),) * size,
        in_specs=[spec(SMEM)] + [spec(VMEM)] * 2 + [spec(HBM)] * (n + 3 + len(extra)),
        out_specs=(spec(VMEM),) * size,
        scratch_shapes=[
            VMEM((tokens, width), BF16),
            VMEM(wg.shape, BF16),
            VMEM(wu.shape, BF16),
            VMEM(wd.shape, BF16),
            VMEM((PICK, width), BF16),
            VMEM((PICK, ff), BF16),
            pltpu.SemaphoreType.DMA((n,)),
            pltpu.SemaphoreType.DMA((3,)),
        ],
        compiler_params=params(48),
        cost_estimate=pl.CostEstimate(
            flops=6 * PICK * width * ff + 4 * PICK * tokens * width, bytes_accessed=18 * MB, transcendentals=0
        ),
        name="experts",
    )(count, slots, gate, *pieces, wg, wu, wd, *extra)


def by_gathers(tokens, gates_to_me, moe_gain, w_gate, w_up, w_down, groups, size, chunks, head_parts):
    z = lax.axis_index("req")
    resident = lax.dynamic_slice_in_dim(tokens, z * ROWS, ROWS, 0)
    starts = [sum(chunks[:c]) for c in range(len(chunks))]
    done = []
    for c, rows in enumerate(chunks):
        parts, marks = head_parts(c)
        if c == 0:
            near = jnp.arange(size, dtype=jnp.int32)[:, None] ^ marks[1]
            far = (marks[2] - jnp.array(ORDER, jnp.int32)[None]) % groups
            near_first = gates_to_me[(far * size + near).reshape(-1)]
        after, moe_in = add_norm(resident[starts[c] : starts[c] + rows], moe_gain[None], along_sum(parts, z, groups))
        done.append((after, along_gather(moe_in, z, groups)))
    last, results = [], []
    for c, rows in enumerate(chunks):
        after, stack = done[c]
        mine = near_first[:, starts[c] : starts[c] + rows].reshape(1, -1)
        at = jnp.arange(mine.shape[1], dtype=jnp.int32)
        routed = mine > 0
        before = jnp.dot(routed.astype(BF16), (at[:, None] < at[None, :]).astype(BF16), preferred_element_type=F32)
        slots = jnp.where(routed, before, -1.0)
        count = jnp.sum(routed.astype(jnp.int32), axis=1)
        made = experts(count, slots, mine, spread(stack, size), w_gate, w_up, w_down, last, size)
        terms, last = gather_sums(made, size)
        cut = {k: add(*(term[i * rows : (i + 1) * rows] for term in terms)) for i, k in enumerate(ORDER)}
        edge = jnp.where(z == 0, cut[1], cut[3])
        parts = along_sum([cut[0], cut[3], cut[2], cut[1], edge], z, groups)
        results.append(add(after, *parts))
    return jnp.concatenate(results), marks[0]


def by_all_to_all(routes, gates, after_attn, moe_in, w_gate, w_up, w_down, experts_n):
    row_count, model_width = moe_in.shape
    top_k = routes.shape[1]
    capacity = 3 * top_k * row_count // (2 * experts_n)
    flat_ids = routes.reshape(-1)
    onehot = (flat_ids[:, None] == jnp.arange(experts_n, dtype=jnp.int32)[None, :]).astype(jnp.int32)
    slots = jnp.sum((jnp.cumsum(onehot, axis=0) - 1) * onehot, axis=1)
    target = flat_ids * capacity + slots
    sources = jnp.arange(row_count * top_k, dtype=jnp.int32) // top_k
    outgoing = jnp.zeros((experts_n * capacity, model_width), BF16).at[target].set(moe_in[sources])
    outgoing = outgoing.reshape(experts_n, capacity, model_width)
    block_in = lax.all_to_all(outgoing, ("req", "exp"), split_axis=0, concat_axis=0, tiled=True)
    flat_rows = block_in.reshape(-1, model_width)
    gate_proj = jnp.dot(flat_rows, w_gate, preferred_element_type=F32)
    up_proj = jnp.dot(flat_rows, w_up, preferred_element_type=F32)
    activated = (jax.nn.silu(gate_proj) * up_proj).astype(BF16)
    produced = jnp.dot(activated, w_down, preferred_element_type=F32).astype(BF16)
    returned = lax.all_to_all(
        produced.reshape(block_in.shape), ("req", "exp"), split_axis=0, concat_axis=0, tiled=True
    )
    picked = returned.reshape(experts_n * capacity, model_width)[target].reshape(row_count, top_k, model_width)
    combined = jnp.sum(picked.astype(F32) * gates[:, :, None], axis=1)
    return (after_attn.astype(F32) + combined).astype(BF16)


def append(cache, fresh, length):
    span = cache.shape[0] + fresh.shape[0]
    padded = jnp.concatenate([cache, jnp.zeros_like(fresh)], axis=0)
    kept_rows = jnp.where(
        (jnp.arange(span, dtype=jnp.int32) < length)[:, None], padded, jnp.zeros_like(padded)
    )
    return lax.dynamic_update_slice(kept_rows, fresh, (length, jnp.zeros((), jnp.int32)))


def body(
    hidden_in,
    cache_keys,
    cache_values,
    cache_len,
    attn_gain,
    w_query,
    w_key,
    w_value,
    q_gain,
    k_gain,
    w_out,
    moe_gain,
    expert_ids,
    expert_gates,
    w_gate,
    w_up,
    w_down,
):
    groups, size = lax.axis_size("req"), lax.axis_size("exp")
    z, e = lax.axis_index("req"), lax.axis_index("exp")
    small = groups == 4 and size == 8
    chunks = CHUNKS if small else (ROWS,)
    tokens = hidden_in[0]
    length = cache_len[0]
    hd = q_gain.shape[0]
    heads = w_query.shape[1] // hd
    marks = jnp.stack([length, e, z]).astype(jnp.int32)

    w_qkv = jnp.concatenate([w_query, w_key, w_value], axis=1)
    qkv_pieces = spread(w_qkv, size)
    out_pieces = spread(stage(w_out, [v for b, _, v in qkv_pieces if not b & 1]), size)

    starts = [sum(chunks[:c]) for c in range(len(chunks))]

    def chunked(array):
        blocks = array.reshape((groups, ROWS) + array.shape[1:])
        parts = [
            blocks[:, at : at + rows].reshape((groups * rows,) + array.shape[1:]) for at, rows in zip(starts, chunks)
        ]
        return jnp.concatenate(parts)

    token_at = chunked(jnp.arange(tokens.shape[0], dtype=jnp.int32))
    frequency = THETA ** (-jnp.arange(hd // 2, dtype=F32) * 2.0 / hd)
    angles = (length + token_at).astype(F32)[:, None] * frequency[None, :]
    cosine, sine = jnp.cos(angles), jnp.sin(angles)
    *q, k_new, v_new = project(
        marks,
        chunked(tokens),
        attn_gain[None],
        jnp.concatenate([cosine, cosine], axis=1),
        jnp.concatenate([-sine, sine], axis=1),
        q_gain[None],
        k_gain[None],
        qkv_pieces,
        size,
        heads,
        chunks,
        groups,
    )
    keep = []

    def head_parts(c):
        att, seen = attend(
            marks, q[c], cache_keys[0], cache_values[0], k_new, v_new, starts[c], chunks[c], heads, keep
        )
        parts = out_project(marks, att, out_pieces, size, groups)
        keep[:] = [parts[0]]
        return parts, seen

    if small:
        ids, gates = expert_ids[0], expert_gates[0]
        number = groups * size
        dense = jnp.sum(
            jnp.where(ids[:, :, None] == jnp.arange(number, dtype=jnp.int32), gates[:, :, None], 0.0), axis=1
        )
        gates_to_me = lax.all_to_all(dense.T, ("req", "exp"), split_axis=0, concat_axis=0, tiled=True)
        result_rows, length = by_gathers(
            tokens, gates_to_me, moe_gain, w_gate[0], w_up[0], w_down[0], groups, size, chunks, head_parts
        )
    else:
        resident = lax.dynamic_slice_in_dim(tokens, z * ROWS, ROWS, 0)
        parts = along_sum(head_parts(0)[0], z, groups)
        after, moe_in = add_norm(resident, moe_gain[None], parts)
        result_rows = by_all_to_all(
            expert_ids[0], expert_gates[0], after, moe_in, w_gate[0], w_up[0], w_down[0], groups * size
        )
    keys_out = append(cache_keys[0], k_new, length)
    values_out = append(cache_values[0], v_new, length)
    return (result_rows[None], keys_out[None], values_out[None])


def solution(mesh):
    placed = (
        P("exp", None, None),
        P("exp", None, "req"),
        P("exp", None, "req"),
        P("exp"),
        P(),
        P("exp", "req"),
        P("exp", "req"),
        P("exp", "req"),
        P(),
        P(),
        P(("req", "exp"), None),
        P(),
        P("exp", "req", None),
        P("exp", "req", None),
        P(("req", "exp"), None, None),
        P(("req", "exp"), None, None),
        P(("req", "exp"), None, None),
    )
    return jax.shard_map(
        body,
        mesh=mesh,
        in_specs=placed,
        out_specs=(P("exp", "req", None), P("exp", None, "req"), P("exp", None, "req")),
        check_vma=False,
    )
```

time: 593 us -> 450 us (0.76)
  blocking collectives: 166 us -> 0 us
  Pallas kernels: 0 us -> 106 us
  starting transfers between devices: 4.2 us -> 110 us
  matrix products: 99.6 us -> 1.62 us
  other arithmetic: 72.5 us -> 34.8 us
  local copies, waits for them, and re-layouts: 56.5 us -> 34.5 us
  waiting for transfers between devices: 171 us -> 156 us
  between operations: 15 us -> 2.63 us
    ppermute x0 -> x76, waiting for transfers between devices: none -> 156 us  [the longest x52 96.1 us: swap(): return lax.ppermute(value, 'exp', [(i, i ^ bit) for i in range(size)])]
    all_to_all x1 -> x0, blocking collectives: 143 us -> none  [body(): lax.all_to_all(outgoing, ('req', 'exp'), split_axis=0, concat_axis=0, til...]
    all_to_all x1, waiting for transfers between devices: 136 us -> 0.26 us  [body(): lax.all_to_all(dense.T, ('req', 'exp'), split_axis=0, concat_axis=0, tile...]
    pallas_call x0 -> x10, Pallas kernels: none -> 106 us  [the longest x2 60.1 us: experts(): pl.pallas_call(functools.partial(expert_kernel, at=at, span=span, extras=...]
    ppermute x0 -> x76, starting transfers between devices: none -> 105 us  [the longest x24 71 us: along(): return lax.ppermute(value, 'req', pairs)]
    dot_general x23 -> x2, matrix products: 99.6 us -> 1.62 us  [by_gathers(): jnp.dot(routed.astype(BF16), (at[:, None] < at[None, :]).astype(BF16), pr...]
    reduce_sum x12 -> x2, other arithmetic: 49.3 us -> 1.34 us  [the longest x1 0.71 us: by_gathers(): count = jnp.sum(routed.astype(jnp.int32), axis=1)]
    reduce_scatter x1 -> x0, waiting for transfers between devices: 33.7 us -> none  [body(): lax.psum_scatter(partial_out.astype(jnp.bfloat16), 'req', scatter_dimensi...]
  transfers between devices with their start and end apart: 4 -> 77, of which waited for: 2 -> 28; matrix products, arithmetic and copies ran while one was open for 27% -> 11% of each run, Pallas kernels for 0% -> 23%
where the time goes in v1:
time: 450 us; the launch traced here: 446 us
  waiting for transfers between devices  156 us (35%)
  starting transfers between devices  110 us (24%)
  Pallas kernels  106 us (24%)
  other arithmetic  34.8 us (8%)
  local copies, waits for them, and re-layouts  34.5 us (8%)
    ppermute x52, waiting for transfers between devices, swap(): return lax.ppermute(value, 'exp', [(i, i ^ bit) for i in range(size)])  96.1 us
    ppermute x24, starting transfers between devices, along(): return lax.ppermute(value, 'req', pairs)  71 us
    pallas_call x2, Pallas kernels, experts(): pl.pallas_call(functools.partial(expert_kernel, at=at, span=span, extras=...  60.1 us
    ppermute x24, waiting for transfers between devices, along(): return lax.ppermute(value, 'req', pairs)  60.1 us
    ppermute x52, starting transfers between devices, swap(): return lax.ppermute(value, 'exp', [(i, i ^ bit) for i in range(size)])  33.8 us
    pallas_call x2, Pallas kernels, attend(): pl.pallas_call(functools.partial(attend_kernel, start=start, rows=rows, h...  26.5 us
    unnamed x112, local copies, waits for them, and re-layouts  18.2 us
    convert_element_type x12, other arithmetic, add(): return total.astype(BF16)  12.1 us
  transfers between devices with their start and end apart: 77, of which 28 were waited for; matrix products, arithmetic and copies ran while one was open for 11% of the time, Pallas kernels for 23%

profile of v1, /device:TPU:0, one launch (start us, length us, event | category | flops | bytes accessed | tf_op | source)
XLA Modules:
  0.0 445.7 jit_solution(585315111070969107)
XLA Ops:
  10.1 13.4 %collective-permute-done.1.rest_2_ = bf16[256,1280]{1,0:T(8,128)(2,1)S(1)} collective-permute-done((bf16[256,1280]{1,0:T(8,128)(2,1)}, bf16[256,1280]{1,0:T(8,128)(2,1)S(1)}, u32[]{:S(2)}, u32[]{:S(2)}) %collective-permute-start.1) | collective-permute-done | bytes 655392 | tf_op jit(solution)/shard_map/ppermute | solution.py:39
  40.5 7.1 %collective-permute-done.10.rest_2_ = bf16[128,2048]{1,0:T(8,128)(2,1)S(1)} collective-permute-done((bf16[128,2048]{1,0:T(8,128)(2,1)}, bf16[128,2048]{1,0:T(8,128)(2,1)S(1)}, u32[]{:S(2)}, u32[]{:S(2)}) %collective-permute-start.10) | collective-permute-done | bytes 524320 | tf_op jit(solution)/shard_map/ppermute | solution.py:39
  63.4 7.1 %project.1 = (bf16[2048,128]{1,0:T(8,128)(2,1)S(1)}, bf16[2048,128]{1,0:T(8,128)(2,1)S(1)}, bf16[512,128]{1,0:T(8,128)(2,1)S(1)}, bf16[512,128]{1,0:T(8,128)(2,1)S(1)}) custom-call(s32[3]{0:T(128)S(1)} %pad_add_fusion.marks, bf16[512,2048]{1,0:T(8,128)(2,1)S(1)} %copy-done.1, f32[1,2048]{1,0:T(1,128)S(1)} %bitcast.64, f32[512,128]{1,0:T(8,128)S(1)} %copy-done.14, ...), custom_call_target="tpu_custom_call" | custom-call | flops 2684354560 | bytes 10485760 | tf_op jit(solution)/shard_map/project/pallas_call | solution.py:179
  71.7 13.2 %attend.2 = (bf16[8,256,128]{2,1,0:T(8,128)(2,1)S(1)}, s32[3]{0:T(128)S(1)}) custom-call(s32[3]{0:T(128)S(1)} %pad_add_fusion.marks, bf16[2048,128]{1,0:T(8,128)(2,1)S(1)} %get-tuple-element.41.q_hbm, bf16[4096,128]{1,0:T(8,128)(2,1)S(1)} %bitcast.50, bf16[4096,128]{1,0:T(8,128)(2,1)S(1)} %bitcast.53, bf16[512,128]{1,0:T(8,128)(2,1)S(1)} %get-tuple-element.42.kn_hbm, ...), custom_call_target="tpu_custom_call" | custom-call | flops 9663676416 | bytes 4194304 | tf_op jit(solution)/shard_map/attend/pallas_call | solution.py:297
  91.3 13.2 %attend.3 = (bf16[8,256,128]{2,1,0:T(8,128)(2,1)S(1)}, s32[3]{0:T(128)S(1)}) custom-call(s32[3]{0:T(128)S(1)} %pad_add_fusion.marks, bf16[2048,128]{1,0:T(8,128)(2,1)S(1)} %get-tuple-element.61.q_hbm, bf16[4096,128]{1,0:T(8,128)(2,1)S(1)} %bitcast.51, bf16[4096,128]{1,0:T(8,128)(2,1)S(1)} %bitcast.54, bf16[512,128]{1,0:T(8,128)(2,1)S(1)} %get-tuple-element.42.kn_hbm, ...), custom_call_target="tpu_custom_call" | custom-call | flops 9663676416 | bytes 4194304 | tf_op jit(solution)/shard_map/attend/pallas_call | solution.py:297
  111.0 4.6 %collective-permute-start.49 = (bf16[64,2048]{1,0:T(8,128)(2,1)S(1)}, bf16[64,2048]{1,0:T(8,128)(2,1)S(1)}, u32[]{:S(2)}, u32[]{:S(2)}) collective-permute-start(bf16[64,2048]{1,0:T(8,128)(2,1)S(1)} %get-tuple-element.67), channel_id=1, source_target_pairs={{0,8},{24,16},{1,9},{25,17},{2,10},{26,18},{3,11},{27,19},{4,12},{... | collective-permute-start | bytes 786440 | tf_op jit(solution)/shard_map/ppermute | solution.py:89
  122.3 7.7 %collective-permute-start.21 = (bf16[64,2048]{1,0:T(8,128)(2,1)S(1)}, bf16[64,2048]{1,0:T(8,128)(2,1)S(1)}, u32[]{:S(2)}, u32[]{:S(2)}) collective-permute-start(bf16[64,2048]{1,0:T(8,128)(2,1)S(1)} %add_convert_fusion.25), channel_id=1, source_target_pairs={{0,16},{8,24},{16,0},{24,8},{1,17},{9,25},{17,1},{25,9},{2,18},{10... | collective-permute-start | bytes 786440 | tf_op jit(solution)/shard_map/ppermute | solution.py:89
  132.1 16.4 %collective-permute-done.21.rest_3_ = bf16[64,2048]{1,0:T(8,128)(2,1)S(1)} collective-permute-done((bf16[64,2048]{1,0:T(8,128)(2,1)S(1)}, bf16[64,2048]{1,0:T(8,128)(2,1)S(1)}, u32[]{:S(2)}, u32[]{:S(2)}) %collective-permute-start.21) | collective-permute-done | bytes 262176 | tf_op jit(solution)/shard_map/ppermute | solution.py:89
  151.6 5.4 %collective-permute-done.50.rest_3_ = bf16[64,2048]{1,0:T(8,128)(2,1)S(1)} collective-permute-done((bf16[64,2048]{1,0:T(8,128)(2,1)S(1)}, bf16[64,2048]{1,0:T(8,128)(2,1)S(1)}, u32[]{:S(2)}, u32[]{:S(2)}) %collective-permute-start.50) | collective-permute-done | bytes 262176 | tf_op jit(solution)/shard_map/ppermute | solution.py:89
  161.3 4.6 %collective-permute-start.24 = (bf16[64,2048]{1,0:T(8,128)(2,1)}, bf16[64,2048]{1,0:T(8,128)(2,1)S(1)}, u32[]{:S(2)}, u32[]{:S(2)}) collective-permute-start(bf16[64,2048]{1,0:T(8,128)(2,1)} %get-tuple-element.52), channel_id=1, source_target_pairs={{0,8},{8,16},{16,24},{1,9},{9,17},{17,25},{2,10},{10,18},{18,26},{... | collective-permute-start | bytes 786440 | tf_op jit(solution)/shard_map/ppermute | solution.py:89
  165.8 5.3 %collective-permute-done.22 = bf16[64,2048]{1,0:T(8,128)(2,1)S(1)} collective-permute-done((bf16[64,2048]{1,0:T(8,128)(2,1)}, bf16[64,2048]{1,0:T(8,128)(2,1)S(1)}, u32[]{:S(2)}, u32[]{:S(2)}) %collective-permute-start.22) | collective-permute-done | bytes 262176 | tf_op jit(solution)/shard_map/ppermute | solution.py:89
  196.5 4.8 %all-to-all-start = ((f32[32,1,128]{2,1,0:T(1,128)}), f32[32,1,128]{2,1,0:T(1,128)S(1)}, u32[]{:S(2)}, u32[]{:S(2)}) async-start(f32[32,1,128]{2,1,0:T(1,128)} %bitcast.17), calls=%async_computation | async-start | bytes 32768 | tf_op jit(solution)/shard_map/all_to_all | solution.py:618
  203.7 7.4 %collective-permute-done.27.rest_2_ = bf16[256,2048]{1,0:T(8,128)(2,1)} collective-permute-done((bf16[256,2048]{1,0:T(8,128)(2,1)S(1)}, bf16[256,2048]{1,0:T(8,128)(2,1)}, u32[]{:S(2)}, u32[]{:S(2)}) %collective-permute-start.27) | collective-permute-done | bytes 1048608 | tf_op jit(solution)/shard_map/ppermute | solution.py:39
  215.3 17.2 %collective-permute-done.56.rest_2_ = bf16[256,2048]{1,0:T(8,128)(2,1)} collective-permute-done((bf16[256,2048]{1,0:T(8,128)(2,1)}, bf16[256,2048]{1,0:T(8,128)(2,1)}, u32[]{:S(2)}, u32[]{:S(2)}) %collective-permute-start.56) | collective-permute-done | bytes 1048608 | tf_op jit(solution)/shard_map/ppermute | solution.py:39
  234.3 4.6 %collective-permute-done.29.rest_4_ = bf16[128,2048]{1,0:T(8,128)(2,1)S(1)} collective-permute-done((bf16[128,2048]{1,0:T(8,128)(2,1)S(1)}, bf16[128,2048]{1,0:T(8,128)(2,1)S(1)}, u32[]{:S(2)}, u32[]{:S(2)}) %collective-permute-start.29) | collective-permute-done | bytes 524320 | tf_op jit(solution)/shard_map/ppermute | solution.py:39
  249.0 30.1 %experts.2 = (bf16[256,2048]{1,0:T(8,128)(2,1)S(1)}, bf16[256,2048]{1,0:T(8,128)(2,1)}, bf16[256,2048]{1,0:T(8,128)(2,1)S(1)}, bf16[256,2048]{1,0:T(8,128)(2,1)}...) custom-call(s32[1]{0:T(128)} %bitcast.22.count_ref, ...), custom_call_target="tpu_custom_call" | custom-call | flops 10066329600 | bytes 18874368 | tf_op jit(solution)/shard_map/experts/pallas_call | solution.py:454
  291.2 30.0 %experts.3 = (bf16[256,2048]{1,0:T(8,128)(2,1)S(1)}, bf16[256,2048]{1,0:T(8,128)(2,1)}, bf16[256,2048]{1,0:T(8,128)(2,1)S(1)}, bf16[256,2048]{1,0:T(8,128)(2,1)}...) custom-call(s32[1]{0:T(128)} %bitcast.29.count_ref, ...), custom_call_target="tpu_custom_call" | custom-call | flops 10066329600 | bytes 18874368 | tf_op jit(solution)/shard_map/experts/pallas_call | solution.py:454
  326.4 9.8 %collective-permute-done.41 = bf16[128,2048]{1,0:T(8,128)(2,1)S(1)} collective-permute-done((bf16[128,2048]{1,0:T(8,128)(2,1)S(1)}, bf16[128,2048]{1,0:T(8,128)(2,1)S(1)}, u32[]{:S(2)}, u32[]{:S(2)}) %collective-permute-start.41) | collective-permute-done | bytes 524320 | tf_op jit(solution)/shard_map/ppermute | solution.py:39
  341.1 10.0 %collective-permute-done.67 = bf16[128,2048]{1,0:T(8,128)(2,1)S(1)} collective-permute-done((bf16[128,2048]{1,0:T(8,128)(2,1)S(1)}, bf16[128,2048]{1,0:T(8,128)(2,1)S(1)}, u32[]{:S(2)}, u32[]{:S(2)}) %collective-permute-start.67) | collective-permute-done | bytes 524320 | tf_op jit(solution)/shard_map/ppermute | solution.py:39
  354.8 15.2 %collective-permute-done.70 = bf16[128,2048]{1,0:T(8,128)(2,1)S(1)} collective-permute-done((bf16[128,2048]{1,0:T(8,128)(2,1)S(1)}, bf16[128,2048]{1,0:T(8,128)(2,1)S(1)}, u32[]{:S(2)}, u32[]{:S(2)}) %collective-permute-start.70) | collective-permute-done | bytes 524320 | tf_op jit(solution)/shard_map/ppermute | solution.py:39
  381.7 13.4 %collective-permute-start.45 = (bf16[64,2048]{1,0:T(8,128)(2,1)S(1)}, bf16[64,2048]{1,0:T(8,128)(2,1)S(1)}, u32[]{:S(2)}, u32[]{:S(2)}) collective-permute-start(bf16[64,2048]{1,0:T(8,128)(2,1)S(1)} %get-tuple-element.79), channel_id=1, source_target_pairs={{0,8},{24,16},{1,9},{25,17},{2,10},{26,18},{3,11},{27,19},{4,12},{... | collective-permute-start | bytes 786440 | tf_op jit(solution)/shard_map/ppermute | solution.py:89
  399.5 11.8 %collective-permute-start.74 = (bf16[64,2048]{1,0:T(8,128)(2,1)S(1)}, bf16[64,2048]{1,0:T(8,128)(2,1)S(1)}, u32[]{:S(2)}, u32[]{:S(2)}) collective-permute-start(bf16[64,2048]{1,0:T(8,128)(2,1)S(1)} %get-tuple-element.82), channel_id=1, source_target_pairs={{0,8},{24,16},{1,9},{25,17},{2,10},{26,18},{3,11},{27,19},{4,12},{... | collective-permute-start | bytes 786440 | tf_op jit(solution)/shard_map/ppermute | solution.py:89
  420.5 4.6 %collective-permute-start.75 = (bf16[64,2048]{1,0:T(8,128)(2,1)S(1)}, bf16[64,2048]{1,0:T(8,128)(2,1)S(1)}, u32[]{:S(2)}, u32[]{:S(2)}) collective-permute-start(bf16[64,2048]{1,0:T(8,128)(2,1)S(1)} %add_convert_fusion.13), channel_id=1, source_target_pairs={{0,16},{8,24},{16,0},{24,8},{1,17},{9,25},{17,1},{25,9},{2,18},{10... | collective-permute-start | bytes 786440 | tf_op jit(solution)/shard_map/ppermute | solution.py:89
  429.9 13.3 %collective-permute-done.75 = bf16[64,2048]{1,0:T(8,128)(2,1)S(1)} collective-permute-done((bf16[64,2048]{1,0:T(8,128)(2,1)S(1)}, bf16[64,2048]{1,0:T(8,128)(2,1)S(1)}, u32[]{:S(2)}, u32[]{:S(2)}) %collective-permute-start.75) | collective-permute-done | bytes 262176 | tf_op jit(solution)/shard_map/ppermute | solution.py:89
  (321 shorter events, 173.0 us)
Async XLA Ops:
  10.1 44.2 %collective-permute-start.4 = (bf16[256,1280]{1,0:T(8,128)(2,1)}, bf16[256,1280]{1,0:T(8,128)(2,1)}, u32[]{:S(2)}, u32[]{:S(2)}) collective-permute-start(bf16[256,1280]{1,0:T(8,128)(2,1)} %constant_dynamic-update-slice_fusion.rest_0_), channel_id=1, source_target_pairs={{0,1},{1,0},{2,3},{3,2},{4,5},{5,4},{6,7},{7,6},{8,9},{9,8},{10,11... | collective-permute-start | bytes 1966088 | tf_op jit(solution)/shard_map/ppermute | solution.py:39
  57.2 27.7 %collective-permute-start.13 = (bf16[128,2048]{1,0:T(8,128)(2,1)S(1)}, bf16[128,2048]{1,0:T(8,128)(2,1)S(1)}, u32[]{:S(2)}, u32[]{:S(2)}) collective-permute-start(bf16[128,2048]{1,0:T(8,128)(2,1)S(1)} %copy-done), channel_id=1, source_target_pairs={{0,1},{1,0},{2,3},{3,2},{4,5},{5,4},{6,7},{7,6},{8,9},{9,8},{10,11... | collective-permute-start | bytes 1572872 | tf_op jit(solution)/shard_map/ppermute | solution.py:39
  87.8 29.1 %collective-permute-start.20 = (bf16[64,2048]{1,0:T(8,128)(2,1)S(1)}, bf16[64,2048]{1,0:T(8,128)(2,1)S(1)}, u32[]{:S(2)}, u32[]{:S(2)}) collective-permute-start(bf16[64,2048]{1,0:T(8,128)(2,1)S(1)} %get-tuple-element.49), channel_id=1, source_target_pairs={{0,8},{24,16},{1,9},{25,17},{2,10},{26,18},{3,11},{27,19},{4,12},{... | collective-permute-start | bytes 786440 | tf_op jit(solution)/shard_map/ppermute | solution.py:89
  108.4 43.1 %collective-permute-start.47 = (bf16[64,2048]{1,0:T(8,128)(2,1)}, bf16[64,2048]{1,0:T(8,128)(2,1)S(1)}, u32[]{:S(2)}, u32[]{:S(2)}) collective-permute-start(bf16[64,2048]{1,0:T(8,128)(2,1)} %get-tuple-element.64), channel_id=1, source_target_pairs={{0,8},{8,16},{16,24},{1,9},{9,17},{17,25},{2,10},{10,18},{18,26},{... | collective-permute-start | bytes 786440 | tf_op jit(solution)/shard_map/ppermute | solution.py:89
  109.7 41.8 %collective-permute-start.48 = (bf16[64,2048]{1,0:T(8,128)(2,1)S(1)}, bf16[64,2048]{1,0:T(8,128)(2,1)S(1)}, u32[]{:S(2)}, u32[]{:S(2)}) collective-permute-start(bf16[64,2048]{1,0:T(8,128)(2,1)S(1)} %get-tuple-element.65), channel_id=1, source_target_pairs={{8,0},{16,8},{24,16},{9,1},{17,9},{25,17},{10,2},{18,10},{26,18},{... | collective-permute-start | bytes 786440 | tf_op jit(solution)/shard_map/ppermute | solution.py:89
  130.2 26.8 %collective-permute-start.50 = (bf16[64,2048]{1,0:T(8,128)(2,1)S(1)}, bf16[64,2048]{1,0:T(8,128)(2,1)S(1)}, u32[]{:S(2)}, u32[]{:S(2)}) collective-permute-start(bf16[64,2048]{1,0:T(8,128)(2,1)S(1)} %add_convert_fusion.18), channel_id=1, source_target_pairs={{0,16},{8,24},{16,0},{24,8},{1,17},{9,25},{17,1},{25,9},{2,18},{10... | collective-permute-start | bytes 786440 | tf_op jit(solution)/shard_map/ppermute | solution.py:89
  184.7 26.4 %collective-permute-start.27 = (bf16[256,2048]{1,0:T(8,128)(2,1)S(1)}, bf16[256,2048]{1,0:T(8,128)(2,1)}, u32[]{:S(2)}, u32[]{:S(2)}) collective-permute-start(bf16[256,2048]{1,0:T(8,128)(2,1)S(1)} %pad_maximum_fusion.1.rest_0_), channel_id=1, source_target_pairs={{0,4},{1,5},{2,6},{3,7},{4,0},{5,1},{6,2},{7,3},{8,12},{9,13},{10,... | collective-permute-start | bytes 3145736 | tf_op jit(solution)/shard_map/ppermute | solution.py:39
  185.8 27.3 %collective-permute-start.26 = (bf16[256,2048]{1,0:T(8,128)(2,1)S(1)}, bf16[256,2048]{1,0:T(8,128)(2,1)}, u32[]{:S(2)}, u32[]{:S(2)}) collective-permute-start(bf16[256,2048]{1,0:T(8,128)(2,1)S(1)} %pad_maximum_fusion.1.rest_0_), channel_id=1, source_target_pairs={{0,2},{1,3},{2,0},{3,1},{4,6},{5,7},{6,4},{7,5},{8,10},{9,11},{10,... | collective-permute-start | bytes 3145736 | tf_op jit(solution)/shard_map/ppermute | solution.py:39
  193.9 38.6 %collective-permute-start.56 = (bf16[256,2048]{1,0:T(8,128)(2,1)}, bf16[256,2048]{1,0:T(8,128)(2,1)}, u32[]{:S(2)}, u32[]{:S(2)}) collective-permute-start(bf16[256,2048]{1,0:T(8,128)(2,1)} %pad_maximum_fusion.4.rest_0_), channel_id=1, source_target_pairs={{0,4},{1,5},{2,6},{3,7},{4,0},{5,1},{6,2},{7,3},{8,12},{9,13},{10,... | collective-permute-start | bytes 3145736 | tf_op jit(solution)/shard_map/ppermute | solution.py:39
  195.0 38.3 %collective-permute-start.55 = (bf16[256,2048]{1,0:T(8,128)(2,1)}, bf16[256,2048]{1,0:T(8,128)(2,1)}, u32[]{:S(2)}, u32[]{:S(2)}) collective-permute-start(bf16[256,2048]{1,0:T(8,128)(2,1)} %pad_maximum_fusion.4.rest_0_), channel_id=1, source_target_pairs={{0,2},{1,3},{2,0},{3,1},{4,6},{5,7},{6,4},{7,5},{8,10},{9,11},{10,... | collective-permute-start | bytes 3145736 | tf_op jit(solution)/shard_map/ppermute | solution.py:39
  196.5 37.1 %all-to-all-start = ((f32[32,1,128]{2,1,0:T(1,128)}), f32[32,1,128]{2,1,0:T(1,128)S(1)}, u32[]{:S(2)}, u32[]{:S(2)}) async-start(f32[32,1,128]{2,1,0:T(1,128)} %bitcast.17), calls=%async_computation | async-start | bytes 32768 | tf_op jit(solution)/shard_map/all_to_all | solution.py:618
  203.4 40.0 %collective-permute-start.30 = (bf16[256,2048]{1,0:T(8,128)(2,1)S(1)}, bf16[256,2048]{1,0:T(8,128)(2,1)}, u32[]{:S(2)}, u32[]{:S(2)}) collective-permute-start(bf16[256,2048]{1,0:T(8,128)(2,1)S(1)} %pad_maximum_fusion.1.rest_0_), channel_id=1, source_target_pairs={{0,1},{1,0},{2,3},{3,2},{4,5},{5,4},{6,7},{7,6},{8,9},{9,8},{10,11... | collective-permute-start | bytes 3145736 | tf_op jit(solution)/shard_map/ppermute | solution.py:39
  212.2 26.7 %collective-permute-start.29 = (bf16[128,2048]{1,0:T(8,128)(2,1)S(1)}, bf16[128,2048]{1,0:T(8,128)(2,1)S(1)}, u32[]{:S(2)}, u32[]{:S(2)}) collective-permute-start(bf16[128,2048]{1,0:T(8,128)(2,1)S(1)} %slice.318), channel_id=1, source_target_pairs={{0,2},{1,3},{2,0},{3,1},{4,6},{5,7},{6,4},{7,5},{8,10},{9,11},{10,... | collective-permute-start | bytes 1572872 | tf_op jit(solution)/shard_map/ppermute | solution.py:39
  243.4 38.4 %collective-permute-start.59 = (bf16[256,2048]{1,0:T(8,128)(2,1)}, bf16[256,2048]{1,0:T(8,128)(2,1)S(1)}, u32[]{:S(2)}, u32[]{:S(2)}) collective-permute-start(bf16[256,2048]{1,0:T(8,128)(2,1)} %pad_maximum_fusion.4.rest_0_), channel_id=1, source_target_pairs={{0,1},{1,0},{2,3},{3,2},{4,5},{5,4},{6,7},{7,6},{8,9},{9,8},{10,11... | collective-permute-start | bytes 3145736 | tf_op jit(solution)/shard_map/ppermute | solution.py:39
  244.2 34.9 %collective-permute-start.58 = (bf16[128,2048]{1,0:T(8,128)(2,1)S(1)}, bf16[128,2048]{1,0:T(8,128)(2,1)S(1)}, u32[]{:S(2)}, u32[]{:S(2)}) collective-permute-start(bf16[128,2048]{1,0:T(8,128)(2,1)S(1)} %slice.339), channel_id=1, source_target_pairs={{0,2},{1,3},{2,0},{3,1},{4,6},{5,7},{6,4},{7,5},{8,10},{9,11},{10,... | collective-permute-start | bytes 1572872 | tf_op jit(solution)/shard_map/ppermute | solution.py:39
  245.9 34.6 %collective-permute-start.57 = (bf16[128,2048]{1,0:T(8,128)(2,1)S(1)}, bf16[128,2048]{1,0:T(8,128)(2,1)S(1)}, u32[]{:S(2)}, u32[]{:S(2)}) collective-permute-start(bf16[128,2048]{1,0:T(8,128)(2,1)S(1)} %slice.338), channel_id=1, source_target_pairs={{0,4},{1,5},{2,6},{3,7},{4,0},{5,1},{6,2},{7,3},{8,12},{9,13},{10,... | collective-permute-start | bytes 1572872 | tf_op jit(solution)/shard_map/ppermute | solution.py:39
  287.9 34.2 %collective-permute-start.38 = (bf16[128,2048]{1,0:T(8,128)(2,1)S(1)}, bf16[128,2048]{1,0:T(8,128)(2,1)S(1)}, u32[]{:S(2)}, u32[]{:S(2)}) collective-permute-start(bf16[128,2048]{1,0:T(8,128)(2,1)S(1)} %get-tuple-element.91), channel_id=1, source_target_pairs={{0,4},{1,5},{2,6},{3,7},{4,0},{5,1},{6,2},{7,3},{8,12},{9,13},{10,... | collective-permute-start | bytes 1572872 | tf_op jit(solution)/shard_map/ppermute | solution.py:39
  321.5 74.9 %collective-permute-start.64 = (bf16[256,2048]{1,0:T(8,128)(2,1)}, bf16[256,2048]{1,0:T(8,128)(2,1)}, u32[]{:S(2)}, u32[]{:S(2)}) collective-permute-start(bf16[256,2048]{1,0:T(8,128)(2,1)} %get-tuple-element.71), channel_id=1, source_target_pairs={{0,1},{1,0},{2,3},{3,2},{4,5},{5,4},{6,7},{7,6},{8,9},{9,8},{10,11... | collective-permute-start | bytes 3145736 | tf_op jit(solution)/shard_map/ppermute | solution.py:39
  322.1 30.7 %collective-permute-start.69 = (bf16[256,2048]{1,0:T(8,128)(2,1)}, bf16[256,2048]{1,0:T(8,128)(2,1)S(1)}, u32[]{:S(2)}, u32[]{:S(2)}) collective-permute-start(bf16[256,2048]{1,0:T(8,128)(2,1)} %get-tuple-element.77), channel_id=1, source_target_pairs={{0,1},{1,0},{2,3},{3,2},{4,5},{5,4},{6,7},{7,6},{8,9},{9,8},{10,11... | collective-permute-start | bytes 3145736 | tf_op jit(solution)/shard_map/ppermute | solution.py:39
  324.3 55.7 %collective-permute-start.39 = (bf16[256,2048]{1,0:T(8,128)(2,1)S(1)}, bf16[256,2048]{1,0:T(8,128)(2,1)}, u32[]{:S(2)}, u32[]{:S(2)}) collective-permute-start(bf16[256,2048]{1,0:T(8,128)(2,1)S(1)} %pad_maximum_fusion.2), channel_id=1, source_target_pairs={{0,2},{1,3},{2,0},{3,1},{4,6},{5,7},{6,4},{7,5},{8,10},{9,11},{10,... | collective-permute-start | bytes 3145736 | tf_op jit(solution)/shard_map/ppermute | solution.py:39
  340.2 39.8 %collective-permute-start.42 = (bf16[256,2048]{1,0:T(8,128)(2,1)}, bf16[256,2048]{1,0:T(8,128)(2,1)}, u32[]{:S(2)}, u32[]{:S(2)}) collective-permute-start(bf16[256,2048]{1,0:T(8,128)(2,1)} %pad_maximum_fusion.3), channel_id=1, source_target_pairs={{0,4},{1,5},{2,6},{3,7},{4,0},{5,1},{6,2},{7,3},{8,12},{9,13},{10,... | collective-permute-start | bytes 3145736 | tf_op jit(solution)/shard_map/ppermute | solution.py:39
  352.8 44.9 %collective-permute-start.68 = (bf16[256,2048]{1,0:T(8,128)(2,1)}, bf16[256,2048]{1,0:T(8,128)(2,1)}, u32[]{:S(2)}, u32[]{:S(2)}) collective-permute-start(bf16[256,2048]{1,0:T(8,128)(2,1)} %pad_maximum_fusion.5), channel_id=1, source_target_pairs={{0,2},{1,3},{2,0},{3,1},{4,6},{5,7},{6,4},{7,5},{8,10},{9,11},{10,... | collective-permute-start | bytes 3145736 | tf_op jit(solution)/shard_map/ppermute | solution.py:39
  381.7 29.5 %collective-permute-start.45 = (bf16[64,2048]{1,0:T(8,128)(2,1)S(1)}, bf16[64,2048]{1,0:T(8,128)(2,1)S(1)}, u32[]{:S(2)}, u32[]{:S(2)}) collective-permute-start(bf16[64,2048]{1,0:T(8,128)(2,1)S(1)} %get-tuple-element.79), channel_id=1, source_target_pairs={{0,8},{24,16},{1,9},{25,17},{2,10},{26,18},{3,11},{27,19},{4,12},{... | collective-permute-start | bytes 786440 | tf_op jit(solution)/shard_map/ppermute | solution.py:89
  396.4 28.8 %collective-permute-start.44 = (bf16[64,2048]{1,0:T(8,128)(2,1)S(1)}, bf16[64,2048]{1,0:T(8,128)(2,1)S(1)}, u32[]{:S(2)}, u32[]{:S(2)}) collective-permute-start(bf16[64,2048]{1,0:T(8,128)(2,1)S(1)} %get-tuple-element.81), channel_id=1, source_target_pairs={{8,0},{16,8},{24,16},{9,1},{17,9},{25,17},{10,2},{18,10},{26,18},{... | collective-permute-start | bytes 786440 | tf_op jit(solution)/shard_map/ppermute | solution.py:89
  (108 other events, 1148.0 us)
